TPU v7x, 128 devices: a whole 4x4x4 slice. The times are simulated.
128 devices in a mesh: grp: 2 (over core), own: 64 (over y, z, x).
Axes of the slice: x: 4, y: 4, z: 4, core: 2. Of those that a mesh axis runs over, the one named last changes fastest.
Arguments:
- row_x: bfloat16 [131072, 1024], P(('grp', 'own')), parts along dimension 0, may hold values from -6 to 6
- row_user: int32 [131072, 1], P(('grp', 'own')), parts along dimension 0, may hold values from 0 to 63; in each aligned block of 1024 rows (0 to 1023, 1024 to 2047, ...) at most 32 rows name the same one
- user_owner: int32 [128], P('grp'), parts along dimension 0, may hold values from 0 to 63, each once
- hist_len: int32 [128], P(('grp', 'own')), parts along dimension 0, may hold values from 1 to 1024, 32768 in all
- new_rows: bfloat16 [128, 64, 1024], P(('grp', 'own')), parts along dimension 0, may hold values from -6 to 6
- cache_keys: bfloat16 [128, 1024, 1024], P(('grp', 'own')), parts along dimension 0, may hold values from -6 to 6
- cache_values: bfloat16 [128, 1024, 1024], P(('grp', 'own')), parts along dimension 0, may hold values from -6 to 6
- w_in: bfloat16 [1024, 4096], replicated, may hold values from -0.1875 to 0.1875
- w_out: bfloat16 [1024, 1024], replicated, may hold values from -0.1875 to 0.1875
- w_score: float32 [1024], replicated, may hold values from -0.1875 to 0.1875
Outputs:
- scores: float32 [131072], P(('grp', 'own')), parts along dimension 0
- new_out: bfloat16 [128, 64, 1024], P(('grp', 'own')), parts along dimension 0
There are 2 independent parts, one for each index of `grp`. A program takes and returns all parts, laid end to end along the dimension named above; an argument that names none is the same for every part. Nothing has to cross between parts.
Inputs may be any that keep to these rules, and one draw needn't show every extreme that they name: `row_user`: among the rows of one device no user appears more than 32 times, and some user appears exactly 32 times. `user_owner`: each device index appears once.
All inputs are finite; a program needn't handle non-finite values. No bound on the sum of `hist_len` on one device may be relied on, other than what follows from the above.
Results may differ from a plain program's by a relative error of at most 0.0095.
Values may be sent and summed in bfloat16 or wider, within the bound.
No kernel may reach another device: no remote copies, remote signals or barrier semaphores. Data moves between devices by JAX's collectives and lax.ppermute only.
A program may use at most 128 MiB of HBM per device.

v0:
```python
import jax
import jax.numpy as jnp
from jax import lax
from jax.sharding import PartitionSpec as P

HEADS = 8
NEW = 64


def layer_norm(v):
    mean = jnp.mean(v, axis=-1, keepdims=True)
    cent = v - mean
    var = jnp.mean(cent * cent, axis=-1, keepdims=True)
    return cent * lax.rsqrt(var + 1e-06)


def project(rows, weight):
    normed = layer_norm(rows.astype(jnp.float32)).astype(jnp.bfloat16)
    return jax.nn.silu(jnp.dot(normed, weight, preferred_element_type=jnp.float32)).astype(
        jnp.bfloat16
    )


def attend(query, keys, values, length, new_k, new_v, causal, counts):
    width = query.shape[1]
    heads = HEADS
    size = width // heads
    scale = 1.0 / size**0.5
    block = min(512, keys.shape[0])
    total = query.shape[0]
    qh = query.reshape(total, heads, size)
    blocks_used = (length + block - 1) // block

    def step(b, acc):
        start = b * block
        kb = lax.dynamic_slice_in_dim(keys, start, block, 0).reshape(block, heads, size)
        vb = lax.dynamic_slice_in_dim(values, start, block, 0).reshape(block, heads, size)
        s = jnp.einsum("rhd,khd->rhk", qh, kb, preferred_element_type=jnp.float32) * scale
        valid = start + jnp.arange(block, dtype=jnp.int32) < length
        a = jnp.where(valid[None, None, :], jax.nn.silu(s), 0.0).astype(jnp.bfloat16)
        return acc + jnp.einsum("rhk,khd->rhd", a, vb, preferred_element_type=jnp.float32)

    acc = lax.fori_loop(0, blocks_used, step, jnp.zeros((total, heads, size), jnp.float32))
    nk = new_k.reshape(new_k.shape[0], heads, size)
    nv = new_v.reshape(new_v.shape[0], heads, size)
    s = jnp.einsum("rhd,khd->rhk", qh, nk, preferred_element_type=jnp.float32) * scale
    a = jax.nn.silu(s)
    if causal:
        keep = (
            jnp.arange(new_k.shape[0], dtype=jnp.int32)[None, :]
            <= jnp.arange(total, dtype=jnp.int32)[:, None]
        )
        a = jnp.where(keep[:, None, :], a, 0.0)
    a = a.astype(jnp.bfloat16)
    acc = acc + jnp.einsum("rhk,khd->rhd", a, nv, preferred_element_type=jnp.float32)
    return (acc.reshape(total, width) / counts[:, None]).astype(jnp.bfloat16)


def finish(rows, attention, gate, w_out):
    gated = (layer_norm(attention.astype(jnp.float32)) * gate.astype(jnp.float32)).astype(
        jnp.bfloat16
    )
    return rows.astype(jnp.float32) + jnp.dot(gated, w_out, preferred_element_type=jnp.float32)


def on_device(
    row_x, row_user, user_owner, hist_len, new_rows, cache_keys, cache_values, w_in, w_out, w_score
):
    n_own = lax.axis_size("own")
    rows_here = row_x.shape[0]
    width = row_x.shape[1]
    capacity = max(2, 2 * rows_here // n_own)
    users_all = user_owner.shape[0]
    match_user = row_user[:, 0][:, None] == jnp.arange(users_all, dtype=jnp.int32)[None, :]
    owner = jnp.sum(jnp.where(match_user, user_owner[None, :], 0), axis=1)
    match_owner = (owner[:, None] == jnp.arange(n_own, dtype=jnp.int32)[None, :]).astype(jnp.int32)
    position = jnp.sum((jnp.cumsum(match_owner, axis=0) - 1) * match_owner, axis=1)
    target = owner * capacity + position
    length = hist_len[0]
    keys = cache_keys[0]
    values = cache_values[0]
    proj = project(new_rows[0], w_in)
    new_u = proj[:, 0:width]
    new_v = proj[:, width : 2 * width]
    new_q = proj[:, 2 * width : 3 * width]
    new_k = proj[:, 3 * width :]
    slot_flags = (
        jnp.zeros((n_own * capacity,), jnp.int32).at[target].set(1).reshape(n_own, capacity)
    )
    gate_rows = project(row_x, w_in[:, 0:width])
    query_rows = project(row_x, w_in[:, 2 * width : 3 * width])
    buffer = jnp.zeros((n_own * capacity, width), query_rows.dtype).at[target].set(query_rows)
    piece = (
        lax.all_to_all(
            buffer.reshape(n_own, capacity, width), "own", split_axis=0, concat_axis=0, tiled=True
        ),
        lax.all_to_all(slot_flags, "own", split_axis=0, concat_axis=0, tiled=True),
    )[0]
    flat = piece.reshape(-1, width)
    cand_n = jnp.full((flat.shape[0],), 1.0, jnp.float32) * (length + NEW).astype(jnp.float32)
    result = attend(flat, keys, values, length, new_k, new_v, False, cand_n)
    returned = lax.all_to_all(
        result.reshape(piece.shape), "own", split_axis=0, concat_axis=0, tiled=True
    )
    attention = returned.reshape(n_own * capacity, width)[target]
    out = finish(row_x, attention, gate_rows, w_out)
    scores = jnp.sum(out * w_score[None, :], axis=1)
    new_n = (length + 1 + jnp.arange(NEW, dtype=jnp.int32)).astype(jnp.float32)
    new_att = attend(new_q, keys, values, length, new_k, new_v, True, new_n)
    new_out = finish(new_rows[0], new_att, new_u, w_out).astype(jnp.bfloat16)
    return (scores, new_out[None])


def solution(mesh):
    placed = (
        P(("grp", "own"), None),
        P(("grp", "own"), None),
        P("grp"),
        P(("grp", "own")),
        P(("grp", "own"), None, None),
        P(("grp", "own"), None, None),
        P(("grp", "own"), None, None),
        P(),
        P(),
        P(),
    )
    return jax.shard_map(
        on_device,
        mesh=mesh,
        in_specs=placed,
        out_specs=(P(("grp", "own")), P(("grp", "own"), None, None)),
        check_vma=False,
    )
```

profile of v0, /device:TPU:0, one launch (start us, length us, event | category | flops | bytes accessed | tf_op | source)
XLA Modules:
  0.0 270.2 jit_solution(10420631541988511135)
XLA Ops:
  0.7 4.1 %copy.28 = bf16[1024,1024]{0,1:T(8,128)(2,1)} copy(bf16[1024,1024]{1,0:T(8,128)(2,1)} %param.14) | data formatting | bytes 4194304 | tf_op args[0]
  4.8 2.0 convert_reduce_fusion
  6.8 2.2 fusion.23
  9.1 18.0 %reduce-window.6 = s32[64,8,128]{2,1,0:T(8,128)S(1)} reduce-window(s32[64,8,128]{2,1,0:T(8,128)S(1)} %fusion.70, s32[]{:T(128)} %constant.84.clone.1), window={size=1x1x128 pad=0_0x0_0x127_0}, to_apply=%region_1.2 | reduce-window | flops 8323072 | bytes 524292 | tf_op jit(solution)/shard_map/reduce-window
  27.3 0.1 copy.31
  27.5 0.1 add_add_fusion
  27.8 6.6 %fusion.38 = f32[1024,1024]{1,0:T(8,128)} fusion(bf16[1024,4096]{1,0:T(8,128)(2,1)} %param.21, bf16[1024,1024]{0,1:T(8,128)(2,1)} %copy.28, f32[1024]{0:T(1024)S(1)} %add_rsqrt_fusion.1, f32[1024]{0:T(1024)S(1)} %broadcast_multiply_fusion.1), kind=kOutput, calls=%fused_computation.62 | convolution fusion | flops 2151677952 | bytes 8396800 | tf_op jit(solution)/shard_map/dot_general | solution.py:19
  34.4 9.7 %scatter_custom_fusion = bf16[2048,1024]{1,0:T(8,128)(2,1)} fusion(s32[1024]{0:T(1024)S(1)} %bitcast.205, f32[1024,1024]{1,0:T(8,128)} %fusion.38, f32[]{:T(128)} %constant.95.clone.1, bf16[]{:T(256)} %constant.90.clone.1), kind=kCustom, calls=%fused_computation.58 | custom fusion | flops 5242880 | bytes 8388614 | tf_op jit(solution)/shard_map/scatter | solution.py:92
  44.1 11.9 %all-to-all-start = ((bf16[64,32,1024]{2,1,0:T(8,128)(2,1)}), bf16[64,32,1024]{2,1,0:T(8,128)(2,1)}, u32[]{:S(2)}, u32[]{:S(2)}) async-start(bf16[64,32,1024]{2,1,0:T(8,128)(2,1)} %bitcast.197), calls=%async_computation | async-start | bytes 8388608 | tf_op jit(solution)/shard_map/all_to_all | solution.py:94
  56.8 4.0 %copy.30 = bf16[1,1024,1024]{1,2,0:T(8,128)(2,1)} copy(bf16[1,1024,1024]{2,1,0:T(8,128)(2,1)} %param.19) | data formatting | bytes 4194304 | tf_op args[5]
  60.8 4.0 %copy.29 = bf16[1,1024,1024]{1,2,0:T(8,128)(2,1)} copy(bf16[1,1024,1024]{2,1,0:T(8,128)(2,1)} %param.20) | data formatting | bytes 4194304 | tf_op args[6]
  64.8 0.2 fusion.63
  65.0 5.1 %multiply_convert_fusion.3 = bf16[64,4096]{1,0:T(8,128)(2,1)S(1)} fusion(bf16[1024,4096]{1,0:T(8,128)(2,1)} %param.21, bf16[1,64,1024]{2,1,0:T(8,128)(2,1)S(1)} %copy-done.2, f32[64]{0:T(128)S(1)} %add_rsqrt_fusion.3, f32[64]{0:T(128)S(1)} %broadcast_multiply_fusion.3), kind=kOutput, calls=%fused_computation.73 | convolution fusion | flops 538443776 | bytes 9044480 | tf_op jit(solution)/shard_map/dot_general | solution.py:19
  70.1 0.8 copy-done.5
  70.9 0.7 slice_bitcast_fusion
  71.7 39.2 %all-to-all-done = bf16[64,32,1024]{2,1,0:T(8,128)(2,1)} async-done(((bf16[64,32,1024]{2,1,0:T(8,128)(2,1)}), bf16[64,32,1024]{2,1,0:T(8,128)(2,1)}, u32[]{:S(2)}, u32[]{:S(2)}) %all-to-all-start) | async-done | bytes 4194336 | tf_op jit(solution)/shard_map/all_to_all | solution.py:94
  110.8 3.3 %copy.54 = bf16[256,8,8,128]{3,2,1,0:T(8,128)(2,1)S(1)} copy(bf16[256,8,8,128]{3,1,2,0:T(8,128)(2,1)} %bitcast.36) | data formatting | bytes 8388608
  114.1 3.0 %copy.33 = bf16[2048,8,128]{2,0,1:T(8,128)(2,1)} copy(bf16[2048,8,128]{2,1,0:T(8,128)(2,1)S(1)} %bitcast.198) | data formatting | bytes 8388608 | tf_op jit(solution)/shard_map/while | solution.py:43
  117.2 0.2 copy-done.1
  117.3 4.3 %broadcast_in_dim.58 = f32[2048,8,128]{0,2,1:T(8,128)} broadcast(f32[]{:T(128)} %constant.85.clone.1), dimensions={} | broadcast | bytes 8388612 | tf_op jit(solution)/shard_map/broadcast_in_dim | solution.py:43
  121.6 42.6 %while.20 = (s32[]{:T(128)}, f32[2048,8,128]{0,2,1:T(8,128)}, s32[]{:T(128)}, bf16[1024,1024]{0,1:T(8,128)(2,1)}, s32[]{:T(128)}, /*index=5*/bf16[1024,1024]{0,1...) while((s32[]{:T(128)}, f32[2048,8,128]{0,2,1:T(8,128)}, ...), condition=%wide.region_8.9_spmd, body=%wide.region_7.8_spmd.sunk | while | flops 4355785728 | bytes 27264168 | solution.py:43
  121.6 2.7 %constant_dynamic-slice_fusion.6 = (bf16[512,1024]{0,1:T(8,128)(2,1)S(1)}, bf16[512,1024]{0,1:T(8,128)(2,1)}) fusion(bf16[1024,1024]{0,1:T(8,128)(2,1)} %get-tuple-element.269, s32[]{:T(128)S(6)} %select_n.65, bf16[1024,1024]{0,1:T(8,128)(2,1)} %get-tuple-element.267), kind=kLoop, calls=%fused_computation.11.clone.1 | loop fusion | bytes 4194308 | tf_op jit(solution)/shard_map/while/body/dynamic_slice | solution.py:36
  124.3 0.7 add_compare_fusion.4
  125.0 17.9 %bitcast_add_fusion.3 = f32[2048,8,128]{0,2,1:T(8,128)} fusion(f32[2048,8,128]{0,2,1:T(8,128)} %get-tuple-element.254, bf16[512,8,128]{0,2,1:T(8,128)(2,1)} %bitcast.194, bf16[512,8,128]{0,2,1:T(8,128)(2,1)S(1)} %bitcast.193, bf16[2048,8,128]{2,0,1:T(8,128)(2,1)} %get-tuple-element.270, pred[512]{0:T(512)(128)(4,1)S(1)} %add_compare_fusion.4), kind=kOutput, calls=%fused_computation.9.clone.1 | convolution fusion | flops 4355784704 | bytes 23069184 | tf_op jit(solution)/shard_map/while/body/rhk,khd->rhd/dot_general | solution.py:41
  142.9 2.7 constant_dynamic-slice_fusion.6
  145.6 0.7 add_compare_fusion.4
  146.3 17.9 %bitcast_add_fusion.3 = f32[2048,8,128]{0,2,1:T(8,128)} fusion(f32[2048,8,128]{0,2,1:T(8,128)} %get-tuple-element.254, bf16[512,8,128]{0,2,1:T(8,128)(2,1)} %bitcast.194, bf16[512,8,128]{0,2,1:T(8,128)(2,1)S(1)} %bitcast.193, bf16[2048,8,128]{2,0,1:T(8,128)(2,1)} %get-tuple-element.270, pred[512]{0:T(512)(128)(4,1)S(1)} %add_compare_fusion.4), kind=kOutput, calls=%fused_computation.9.clone.1 | convolution fusion | flops 4355784704 | bytes 23069184 | tf_op jit(solution)/shard_map/while/body/rhk,khd->rhd/dot_general | solution.py:41
  164.2 9.8 %fusion.18 = bf16[2048,8,128]{0,2,1:T(8,128)(2,1)} fusion(f32[2048,8,128]{0,2,1:T(8,128)} %get-tuple-element.78, f32[]{:T(128)S(6)} %convert_element_type.103, bf16[8,8,8,128]{3,2,1,0:T(8,128)(2,1)S(1)} %copy-done.6, bf16[8,8,8,128]{3,2,1,0:T(8,128)(2,1)S(1)} %copy-done.7, bf16[2048,8,128]{2,1,0:T(8,128)(2,1)} %bitcast.199), kind=kOutput, calls=%fused_computation.33 | convolution fusion | flops 549453824 | bytes 17039364 | tf_op jit(solution)/shard_map/rhk,khd->rhd/dot_general | solution.py:55
  174.0 6.8 %copy.37 = bf16[2048,8,128]{2,1,0:T(8,128)(2,1)} copy(bf16[2048,8,128]{0,2,1:T(8,128)(2,1)} %fusion.18) | data formatting | bytes 8388608 | tf_op jit(solution)/shard_map/convert_element_type | solution.py:56
  180.8 7.3 %convert_element_type.105 = bf16[64,32,1024]{2,1,0:T(8,128)(2,1)} reshape(bf16[2048,8,128]{2,1,0:T(8,128)(2,1)} %copy.37) | data formatting | bytes 8388608 | tf_op jit(solution)/shard_map/convert_element_type | solution.py:56
  188.1 5.8 %all-to-all-start.1 = ((bf16[64,32,1024]{2,1,0:T(8,128)(2,1)}), bf16[64,32,1024]{2,1,0:T(8,128)(2,1)}, u32[]{:S(2)}, u32[]{:S(2)}) async-start(bf16[64,32,1024]{2,1,0:T(8,128)(2,1)} %convert_element_type.105), calls=%async_computation.1 | async-start | bytes 8388608 | tf_op jit(solution)/shard_map/all_to_all | solution.py:102
  193.9 0.6 add_convert_fusion
  194.5 0.7 broadcast_in_dim.88
  195.3 12.4 %while.21 = (s32[]{:T(128)}, f32[64,8,128]{2,0,1:T(8,128)}, s32[]{:T(128)}, bf16[1024,1024]{0,1:T(8,128)(2,1)}, s32[]{:T(128)}, /*index=5*/bf16[1024,1024]{0,1:T...) while((s32[]{:T(128)}, f32[64,8,128]{2,0,1:T(8,128)}, ...), condition=%wide.region_15.16_spmd, body=%wide.region_14.15_spmd.sunk | while | flops 136119296 | bytes 6948007 | solution.py:43
  195.3 2.8 %constant_dynamic-slice_fusion.7 = (bf16[512,1024]{0,1:T(8,128)(2,1)S(1)}, bf16[512,1024]{0,1:T(8,128)(2,1)}) fusion(bf16[1024,1024]{0,1:T(8,128)(2,1)} %get-tuple-element.302, s32[]{:T(128)S(6)} %select_n.67, bf16[1024,1024]{0,1:T(8,128)(2,1)} %get-tuple-element.300), kind=kLoop, calls=%fused_computation.26.clone.1 | loop fusion | bytes 4194308 | tf_op jit(solution)/shard_map/while/body/dynamic_slice | solution.py:36
  198.0 0.7 add_compare_fusion.5
  198.7 2.8 %fusion.131 = f32[64,8,128]{2,0,1:T(8,128)} fusion(f32[64,8,128]{2,0,1:T(8,128)} %get-tuple-element.287, bf16[512,8,128]{0,2,1:T(8,128)(2,1)} %bitcast.196, bf16[64,8,128]{2,0,1:T(8,128)(2,1)S(1)} %get-tuple-element.303, bf16[512,8,128]{0,2,1:T(8,128)(2,1)S(1)} %bitcast.195, pred[512]{0:T(512)(128)(4,1)S(1)} %add_compare_fusion.5), kind=kOutput, calls=%fused_computation.19.clone.1 | convolution fusion | flops 136118272 | bytes 2753024 | tf_op jit(solution)/shard_map/while/body/rhk,khd->rhd/dot_general | solution.py:41
  201.5 2.7 %constant_dynamic-slice_fusion.7 = (bf16[512,1024]{0,1:T(8,128)(2,1)S(1)}, bf16[512,1024]{0,1:T(8,128)(2,1)}) fusion(bf16[1024,1024]{0,1:T(8,128)(2,1)} %get-tuple-element.302, s32[]{:T(128)S(6)} %select_n.67, bf16[1024,1024]{0,1:T(8,128)(2,1)} %get-tuple-element.300), kind=kLoop, calls=%fused_computation.26.clone.1 | loop fusion | bytes 4194308 | tf_op jit(solution)/shard_map/while/body/dynamic_slice | solution.py:36
  204.2 0.7 add_compare_fusion.5
  204.9 2.8 %fusion.131 = f32[64,8,128]{2,0,1:T(8,128)} fusion(f32[64,8,128]{2,0,1:T(8,128)} %get-tuple-element.287, bf16[512,8,128]{0,2,1:T(8,128)(2,1)} %bitcast.196, bf16[64,8,128]{2,0,1:T(8,128)(2,1)S(1)} %get-tuple-element.303, bf16[512,8,128]{0,2,1:T(8,128)(2,1)S(1)} %bitcast.195, pred[512]{0:T(512)(128)(4,1)S(1)} %add_compare_fusion.5), kind=kOutput, calls=%fused_computation.19.clone.1 | convolution fusion | flops 136118272 | bytes 2753024 | tf_op jit(solution)/shard_map/while/body/rhk,khd->rhd/dot_general | solution.py:41
  207.6 1.6 convert_reduce_fusion.2
  209.2 0.2 fusion.66
  209.5 2.1 fusion.59
  211.6 35.7 %all-to-all-done.1 = bf16[64,32,1024]{2,1,0:T(8,128)(2,1)} async-done(((bf16[64,32,1024]{2,1,0:T(8,128)(2,1)}), bf16[64,32,1024]{2,1,0:T(8,128)(2,1)}, u32[]{:S(2)}, u32[]{:S(2)}) %all-to-all-start.1) | async-done | bytes 4194336 | tf_op jit(solution)/shard_map/all_to_all | solution.py:102
  247.3 8.8 %gather_fusion = bf16[1024,1024]{1,0:T(8,128)(2,1)} fusion(bf16[2048,1024]{1,0:T(8,128)(2,1)} %bitcast.21, s32[1024]{0:T(1024)S(1)} %broadcast_clamp_fusion), kind=kCustom, calls=%fused_computation | custom fusion | bytes 4198400 | tf_op jit(solution)/shard_map/gather | solution.py:105
  256.1 1.9 convert_reduce_fusion.1
  258.0 2.3 fusion.25
  260.4 9.8 %fusion.29 = f32[1024]{0:T(1024)} fusion(bf16[1024,1024]{0,1:T(8,128)(2,1)} %copy.28, f32[1024]{0:T(1024)S(1)} %copy-done.16, bf16[1024,1024]{1,0:T(8,128)(2,1)S(1)} %copy-done, bf16[1024,1024]{1,0:T(8,128)(2,1)} %gather_fusion, f32[1024]{0:T(1024)S(1)} %add_rsqrt_fusion, f32[1024]{0:T(1024)S(1)} %broadcast_multiply_fusion, bf16[1024,4096]{1,0:T(8,128)(2,1)} %param.21, ...), kind=kOutput, calls=%fused_computation.49 | convolution fusion | flops 4314889216 | bytes 10510336 | tf_op jit(solution)/shard_map/dot_general | solution.py:63
  (53 shorter events, 0.7 us)
Async XLA Ops:
  0.6 208.8 %copy-start = (bf16[1024,1024]{1,0:T(8,128)(2,1)S(1)}, bf16[1024,1024]{1,0:T(8,128)(2,1)}, u32[]{:S(2)}) copy-start(bf16[1024,1024]{1,0:T(8,128)(2,1)} %param.22) | copy-start | bytes 6291460
  0.6 8.3 %copy-start.12 = (s32[1024,1]{0,1:T(1,128)S(1)}, s32[1024,1]{0,1:T(1,128)}, u32[]{:S(2)}) copy-start(s32[1024,1]{0,1:T(1,128)} %param.15) | copy-start | bytes 12292
  0.7 8.3 %copy-start.15 = (s32[64]{0:T(128)S(1)}, s32[64]{0:T(128)}, u32[]{:S(2)}) copy-start(s32[64]{0:T(128)} %param.16) | copy-start | bytes 772
  6.7 27.6 %copy-start.8 = (f32[1024]{0:T(1024)}, f32[1024]{0:T(1024)S(1)}, u32[]{:S(2)}) copy-start(f32[1024]{0:T(1024)S(1)} %broadcast_multiply_fusion.1) | copy-start | bytes 12292
  9.0 25.4 %copy-start.13 = (f32[1024]{0:T(1024)}, f32[1024]{0:T(1024)S(1)}, u32[]{:S(2)}) copy-start(f32[1024]{0:T(1024)S(1)} %add_rsqrt_fusion.1) | copy-start | bytes 12292
  27.8 6.6 %copy-start.10 = (s32[1024,1]{0,1:T(1,128)}, s32[1024,1]{0,1:T(1,128)S(1)}, u32[]{:S(2)}) copy-start(s32[1024,1]{0,1:T(1,128)S(1)} %compare_select_fusion) | copy-start | bytes 12292
  44.1 66.7 %all-to-all-start = ((bf16[64,32,1024]{2,1,0:T(8,128)(2,1)}), bf16[64,32,1024]{2,1,0:T(8,128)(2,1)}, u32[]{:S(2)}, u32[]{:S(2)}) async-start(bf16[64,32,1024]{2,1,0:T(8,128)(2,1)} %bitcast.197), calls=%async_computation | async-start | bytes 8388608 | tf_op jit(solution)/shard_map/all_to_all | solution.py:94
  56.7 8.0 %copy-start.2 = (bf16[1,64,1024]{2,1,0:T(8,128)(2,1)S(1)}, bf16[1,64,1024]{2,1,0:T(8,128)(2,1)}, u32[]{:S(2)}) copy-start(bf16[1,64,1024]{2,1,0:T(8,128)(2,1)} %param.18) | copy-start | bytes 393220
  70.1 0.8 copy-start.5
  114.1 3.2 %copy-start.1 = (bf16[256,8,8,128]{3,2,1,0:T(8,128)(2,1)}, bf16[256,8,8,128]{3,2,1,0:T(8,128)(2,1)S(1)}, u32[]{:S(2)}) copy-start(bf16[256,8,8,128]{3,2,1,0:T(8,128)(2,1)S(1)} %copy.54) | copy-start | bytes 12582916
  121.6 42.6 %copy-start.6 = (bf16[8,8,8,128]{3,2,1,0:T(8,128)(2,1)S(1)}, bf16[8,8,8,128]{3,2,1,0:T(8,128)(2,1)}, u32[]{:S(2)}) copy-start(bf16[8,8,8,128]{3,2,1,0:T(8,128)(2,1)} %get-tuple-element.143) | copy-start | bytes 393220
  121.6 42.6 %copy-start.7 = (bf16[8,8,8,128]{3,2,1,0:T(8,128)(2,1)S(1)}, bf16[8,8,8,128]{3,2,1,0:T(8,128)(2,1)}, u32[]{:S(2)}) copy-start(bf16[8,8,8,128]{3,2,1,0:T(8,128)(2,1)} %get-tuple-element.144) | copy-start | bytes 393220
  188.1 5.8 %copy-start.4 = (bf16[8,8,8,128]{3,2,1,0:T(8,128)(2,1)S(1)}, bf16[8,8,8,128]{3,2,1,0:T(8,128)(2,1)}, u32[]{:S(2)}) copy-start(bf16[8,8,8,128]{3,2,1,0:T(8,128)(2,1)} %get-tuple-element.142) | copy-start | bytes 393220
  188.1 59.2 %all-to-all-start.1 = ((bf16[64,32,1024]{2,1,0:T(8,128)(2,1)}), bf16[64,32,1024]{2,1,0:T(8,128)(2,1)}, u32[]{:S(2)}, u32[]{:S(2)}) async-start(bf16[64,32,1024]{2,1,0:T(8,128)(2,1)} %convert_element_type.105), calls=%async_computation.1 | async-start | bytes 8388608 | tf_op jit(solution)/shard_map/all_to_all | solution.py:102
  195.3 14.2 %copy-start.11 = (s32[1024,1]{0,1:T(1,128)S(1)}, s32[1024,1]{0,1:T(1,128)}, u32[]{:S(2)}) copy-start(s32[1024,1]{0,1:T(1,128)} %copy-done.10) | copy-start | bytes 12292
  195.3 14.2 %copy-start.3 = (bf16[1,64,1024]{2,1,0:T(8,128)(2,1)S(1)}, bf16[1,64,1024]{2,1,0:T(8,128)(2,1)}, u32[]{:S(2)}) copy-start(bf16[1,64,1024]{2,1,0:T(8,128)(2,1)} %param.18) | copy-start | bytes 393220
  256.1 4.3 %copy-start.9 = (f32[1024]{0:T(1024)S(1)}, f32[1024]{0:T(1024)}, u32[]{:S(2)}) copy-start(f32[1024]{0:T(1024)} %copy-done.8) | copy-start | bytes 12292
  256.1 4.3 %copy-start.14 = (f32[1024]{0:T(1024)S(1)}, f32[1024]{0:T(1024)}, u32[]{:S(2)}) copy-start(f32[1024]{0:T(1024)} %copy-done.13) | copy-start | bytes 12292
  256.1 4.3 %copy-start.16 = (f32[1024]{0:T(1024)S(1)}, f32[1024]{0:T(1024)}, u32[]{:S(2)}) copy-start(f32[1024]{0:T(1024)} %param.23) | copy-start | bytes 12292
where the time goes:
time: 271 us; the launch traced here: 270 us
  matrix products  76.3 us (28%)
  waiting for transfers between devices  74.9 us (28%)
  local copies, waits for them, and re-layouts  59.3 us (22%)
  other arithmetic  40.3 us (15%)
  starting transfers between devices  17.7 us (7%)
    dot_general x4, matrix products, step(): jnp.einsum('rhk,khd->rhd', a, vb, preferred_element_type=jnp.float32)  41.4 us
    all_to_all x1, waiting for transfers between devices, on_device(): lax.all_to_all(buffer.reshape(n_own, capacity, width), 'own', split_axis=...  39.2 us
    all_to_all x1, waiting for transfers between devices, on_device(): lax.all_to_all(result.reshape(piece.shape), 'own', split_axis=0, concat_a...  35.7 us
    another operation x2, other arithmetic  18 us
    unnamed x39, local copies, waits for them, and re-layouts  17.1 us
    convert_element_type x2, local copies, waits for them, and re-layouts, attend(): return (acc.reshape(total, width) / counts[:, None]).astype(jnp.bfloat16)  14.1 us
    all_to_all x1, starting transfers between devices, on_device(): lax.all_to_all(buffer.reshape(n_own, capacity, width), 'own', split_axis=...  11.9 us
    dot_general x2, matrix products, finish(): jnp.dot(gated, w_out, preferred_element_type=jnp.float32)  11.9 us
  transfers between devices with their start and end apart: 2, of which 2 were waited for; matrix products, arithmetic and copies ran while one was open for 12% of the time, Pallas kernels for 0%

commit v1 on v0

v1 whole, which is shorter than its diff:
```python
import jax
import jax.numpy as jnp
from jax import lax
from jax.experimental import pallas as pl
from jax.experimental.pallas import tpu as pltpu
from jax.sharding import PartitionSpec as P

HEADS = 8
NEW = 64
BF = jnp.bfloat16
F32 = jnp.float32
VMEM_LIMIT = 56 * 1024 * 1024


def dot(a, b, dims=((1,), (0,))):
    return lax.dot_general(a, b, (dims, ((), ())), preferred_element_type=F32)


def normalize(v):
    mean = jnp.mean(v, axis=-1, keepdims=True)
    cent = v - mean
    var = jnp.mean(cent * cent, axis=-1, keepdims=True)
    return cent * lax.rsqrt(var + 1e-06)


def silu(v):
    half = 0.5 * v
    return half + half * jnp.tanh(half)


def split3(v):
    hi = v.astype(BF)
    rest = v - hi.astype(F32)
    mid = rest.astype(BF)
    low = (rest - mid.astype(F32)).astype(BF)
    return hi, mid, low


def split_rows(row):
    width = row.shape[1]
    hi, mid, low = split3(row)
    place = lax.broadcasted_iota(jnp.int32, (8, width), 0)
    parts = jnp.where(place == 0, hi.astype(F32), 0.0)
    parts = jnp.where(place == 1, mid.astype(F32), parts)
    return jnp.where(place == 2, low.astype(F32), parts).astype(BF)


def fill(out_ref, slots, first, owner, position, normed_ref):
    rows = normed_ref.shape[0]
    inside = jnp.logical_and(position >= first, position < first + slots)
    key = jnp.where(inside, owner * slots + position - first, -1)
    step = 256
    for b in range(out_ref.shape[0] // step):
        at = lax.broadcasted_iota(jnp.int32, (step, rows), 0) + b * step
        pick = jnp.where(at == key, 1.0, 0.0).astype(BF)
        out_ref[b * step : (b + 1) * step, :] = dot(pick, normed_ref[...]).astype(BF)


def route_kernel(
    slots, x_ref, user_ref, owner_ref, score_ref, buf_ref, normed_ref, place_ref, base_ref
):
    rows, width = x_ref.shape
    users = owner_ref.shape[1]
    step = 128
    for b in range(rows // step):
        part = slice(b * step, (b + 1) * step)
        normed_ref[part, :] = normalize(x_ref[part, :].astype(F32)).astype(BF)
    along = lax.broadcasted_iota(jnp.int32, (users, users), 0)
    across = lax.broadcasted_iota(jnp.int32, (users, users), 1)
    owners = jnp.sum(
        jnp.where(along == across, owner_ref[...], 0).astype(F32), axis=1, keepdims=True
    )
    before = lax.broadcasted_iota(jnp.int32, (step, step), 0) < lax.broadcasted_iota(
        jnp.int32, (step, step), 1
    )
    before = jnp.where(before, 1.0, 0.0).astype(BF)
    seen = jnp.zeros((users, 1), F32)
    for b in range(rows // step):
        part = slice(b * step, (b + 1) * step)
        match = lax.broadcasted_iota(jnp.int32, (users, step), 0) == user_ref[:, part]
        match = jnp.where(match, 1.0, 0.0)
        earlier = dot(match.astype(BF), before) + seen
        seen = seen + jnp.sum(match, axis=1, keepdims=True)
        position = jnp.sum(earlier * match, axis=0, keepdims=True)
        owner = jnp.sum(owners * match, axis=0, keepdims=True)
        place_ref[0:1, part] = owner.astype(jnp.int32)
        place_ref[1:2, part] = position.astype(jnp.int32)
    base = dot(split_rows(score_ref[...]), x_ref[...], ((1,), (1,)))
    base_ref[...] = jnp.sum(base, axis=0, keepdims=True)
    fill(buf_ref, slots, 0, place_ref[0:1, :], place_ref[1:2, :], normed_ref)


def fill_kernel(slots, first, place_ref, normed_ref, buf_ref):
    fill(buf_ref, slots, first, place_ref[0:1, :], place_ref[1:2, :], normed_ref)


def new_kernel(
    length_ref, new_ref, w_in_ref, keys_ref, values_ref, w_out_ref, score_ref,
    k_ref, v_ref, vec_ref, out_ref,
):
    length = length_ref[0]
    fresh, width = new_ref.shape
    hist = keys_ref.shape[0]
    size = width // HEADS
    rows = new_ref[...].astype(F32)
    normed = normalize(rows).astype(BF)
    cut = [
        silu(dot(normed, w_in_ref[:, i * width : (i + 1) * width])).astype(BF) for i in range(4)
    ]
    gate, value, query, key = cut
    k_ref[0:hist, :] = keys_ref[...]
    k_ref[hist : hist + fresh, :] = key
    for b in range(0, hist, 128):
        at = lax.broadcasted_iota(jnp.int32, (128, width), 0) + b
        kept = jnp.where(at < length, values_ref[b : b + 128, :].astype(F32), 0.0)
        v_ref[b : b + 128, :] = kept.astype(BF)
    v_ref[hist : hist + fresh, :] = value
    vec = jnp.sum(dot(split_rows(score_ref[...]), w_out_ref[...], ((1,), (1,))), axis=0, keepdims=True)
    vec_ref[...] = split_rows(vec)
    total = hist + fresh
    at = lax.broadcasted_iota(jnp.int32, (fresh, total), 1)
    line = lax.broadcasted_iota(jnp.int32, (fresh, total), 0)
    keep = at <= line + hist
    outs = []
    for h in range(HEADS):
        cols = slice(h * size, (h + 1) * size)
        s = dot(query[:, cols], k_ref[:, cols], ((1,), (1,))) * (1.0 / size**0.5)
        a = jnp.where(keep, silu(s), 0.0).astype(BF)
        outs.append(dot(a, v_ref[:, cols]))
    number = lax.broadcasted_iota(jnp.int32, (fresh, 1), 0) + (length + 1)
    att = (jnp.concatenate(outs, axis=1) / number.astype(F32)).astype(BF)
    gated = (normalize(att.astype(F32)) * gate.astype(F32)).astype(BF)
    out_ref[...] = (rows + dot(gated, w_out_ref[...])).astype(BF)


def rank_kernel(slots, first, length_ref, x_ref, wq_ref, wu_ref, k_ref, v_ref, vec_ref, out_ref):
    count, width = x_ref.shape
    size = width // HEADS
    x = x_ref[...]
    query = (silu(dot(x, wq_ref[...])) * (0.5 / size**0.5)).astype(BF)
    outs = []
    for h in range(HEADS):
        cols = slice(h * size, (h + 1) * size)
        s = dot(query[:, cols], k_ref[:, cols], ((1,), (1,)))
        a = (s + s * jnp.tanh(s)).astype(BF)
        outs.append(dot(a, v_ref[:, cols]))
    number = (length_ref[0] + NEW).astype(F32)
    att = (jnp.concatenate(outs, axis=1) / number).astype(BF)
    gate = silu(dot(x, wu_ref[...])).astype(BF)
    gated = (normalize(att.astype(F32)) * gate.astype(F32)).astype(BF)
    line = jnp.sum(dot(vec_ref[...], gated, ((1,), (1,))), axis=0, keepdims=True)
    groups = count // slots
    at = lax.broadcasted_iota(jnp.int32, (groups, count), 1)
    group = lax.broadcasted_iota(jnp.int32, (groups, count), 0)
    mine = jnp.logical_and(at >= group * slots, at < (group + 1) * slots)
    row = lax.broadcasted_iota(jnp.int32, (count, 128), 0)
    lane = lax.broadcasted_iota(jnp.int32, (count, 128), 1)
    spread = jnp.where(lax.rem(row, slots) + first == lane, 1.0, 0.0).astype(BF)
    total = jnp.zeros((groups, 128), F32)
    for part in split3(line):
        total += dot(jnp.where(mine, part.astype(F32), 0.0).astype(BF), spread)
    out_ref[...] = total


def score_kernel(place_ref, base_ref, ret_ref, out_ref):
    parties, lanes = ret_ref.shape
    rows = base_ref.shape[1]
    owner = place_ref[0:1, :]
    position = place_ref[1:2, :]
    match = lax.broadcasted_iota(jnp.int32, (parties, rows), 0) == owner
    match = jnp.where(match, 1.0, 0.0).astype(BF)
    got = jnp.zeros((lanes, rows), F32)
    for part in split3(ret_ref[...]):
        got += dot(part, match, ((0,), (0,)))
    slot = lax.broadcasted_iota(jnp.int32, (lanes, rows), 0) == position
    out_ref[...] = base_ref[...] + jnp.sum(jnp.where(slot, got, 0.0), axis=0, keepdims=True)


def whole(n):
    return [pl.BlockSpec(memory_space=pltpu.VMEM)] * n


def params():
    return pltpu.CompilerParams(vmem_limit_bytes=VMEM_LIMIT)


def cost(macs, moved, transcendentals=0):
    return pl.CostEstimate(flops=2 * macs, bytes_accessed=moved, transcendentals=transcendentals)


def on_device(
    row_x, row_user, user_owner, hist_len, new_rows, cache_keys, cache_values, w_in, w_out, w_score
):
    n_own = lax.axis_size("own")
    rows, width = row_x.shape
    users = user_owner.shape[0]
    hist = cache_keys.shape[1]
    total = hist + NEW
    capacity = 2 * rows // n_own
    chunks = (capacity // 2, capacity // 2)
    score_row = w_score.reshape(1, width)
    sds = jax.ShapeDtypeStruct

    def all_to_all(v):
        return lax.all_to_all(v, "own", split_axis=0, concat_axis=0, tiled=True)

    buf, normed, place, base = pl.pallas_call(
        lambda *refs: route_kernel(chunks[0], *refs),
        out_shape=(
            sds((n_own * chunks[0], width), BF),
            sds((rows, width), BF),
            sds((2, rows), jnp.int32),
            sds((1, rows), F32),
        ),
        in_specs=whole(4),
        out_specs=tuple(whole(4)),
        compiler_params=params(),
        cost_estimate=cost(rows * width * n_own * chunks[0], 3 * 2 * rows * width),
        name="route",
    )(row_x, row_user.reshape(1, rows), user_owner.reshape(1, users), score_row)

    pieces = [all_to_all(buf.reshape(n_own, chunks[0], width))]
    first = chunks[0]
    for slots in chunks[1:]:
        buf = pl.pallas_call(
            lambda *refs, slots=slots, first=first: fill_kernel(slots, first, *refs),
            out_shape=sds((n_own * slots, width), BF),
            in_specs=whole(2),
            out_specs=whole(1)[0],
            compiler_params=params(),
            cost_estimate=cost(rows * width * n_own * slots, 2 * 2 * rows * width),
            name="fill",
        )(place, normed)
        pieces.append(all_to_all(buf.reshape(n_own, slots, width)))
        first += slots

    keys, values, vec, new_out = pl.pallas_call(
        new_kernel,
        out_shape=(
            sds((total, width), BF),
            sds((total, width), BF),
            sds((8, width), BF),
            sds((NEW, width), BF),
        ),
        in_specs=[pl.BlockSpec(memory_space=pltpu.SMEM)] + whole(6),
        out_specs=tuple(whole(4)),
        compiler_params=params(),
        cost_estimate=cost(8 * NEW * width * width, 20 * width * width),
        name="fresh",
    )(hist_len, new_rows[0], w_in, cache_keys[0], cache_values[0], w_out, score_row)

    tile = 256
    result = None
    first = 0
    for piece, slots in zip(pieces, chunks):
        count = n_own * slots
        part = pl.pallas_call(
            lambda *refs, slots=slots, first=first: rank_kernel(slots, first, *refs),
            grid=(count // tile,),
            out_shape=sds((n_own, 128), F32),
            in_specs=[
                pl.BlockSpec(memory_space=pltpu.SMEM),
                pl.BlockSpec((tile, width), lambda i: (i, 0)),
                pl.BlockSpec((width, width), lambda i: (0, 2)),
                pl.BlockSpec((width, width), lambda i: (0, 0)),
                pl.BlockSpec((total, width), lambda i: (0, 0)),
                pl.BlockSpec((total, width), lambda i: (0, 0)),
                pl.BlockSpec((8, width), lambda i: (0, 0)),
            ],
            out_specs=pl.BlockSpec((tile // slots, 128), lambda i: (i, 0)),
            compiler_params=params(),
            cost_estimate=cost(
                count * width * (2 * width + 4 * total), 10 * width * width, count * HEADS * total
            ),
            name="rank",
        )(hist_len, piece.reshape(count, width), w_in, w_in, keys, values, vec)
        result = part if result is None else result + part
        first += slots

    returned = all_to_all(result.reshape(n_own, 1, 128)).reshape(n_own, 128)
    scores = pl.pallas_call(
        score_kernel,
        out_shape=sds((1, rows), F32),
        in_specs=whole(3),
        out_specs=whole(1)[0],
        compiler_params=params(),
        name="scores",
    )(place, base, returned)
    return (scores.reshape(rows), new_out[None])


def solution(mesh):
    placed = (
        P(("grp", "own"), None),
        P(("grp", "own"), None),
        P("grp"),
        P(("grp", "own")),
        P(("grp", "own"), None, None),
        P(("grp", "own"), None, None),
        P(("grp", "own"), None, None),
        P(),
        P(),
        P(),
    )
    return jax.shard_map(
        on_device,
        mesh=mesh,
        in_specs=placed,
        out_specs=(P(("grp", "own")), P(("grp", "own"), None, None)),
        check_vma=False,
    )
```

time: 271 us -> 139 us (0.51)
  matrix products: 76.3 us -> 0 us
  waiting for transfers between devices: 74.9 us -> 0.01 us
  Pallas kernels: 0 us -> 68.1 us
  blocking collectives: 0 us -> 61.9 us
  local copies, waits for them, and re-layouts: 59.3 us -> 1.35 us
  other arithmetic: 40.3 us -> 0.76 us
  starting transfers between devices: 17.7 us -> 4.87 us
    dot_general x10 -> x0, matrix products: 76.3 us -> none  [the longest x4 41.4 us: step(): jnp.einsum('rhk,khd->rhd', a, vb, preferred_element_type=jnp.float32)]
    all_to_all x2 -> x1, waiting for transfers between devices: 74.9 us -> 0.01 us  [all_to_all(): return lax.all_to_all(v, 'own', split_axis=0, concat_axis=0, tiled=True)]
    pallas_call x0 -> x6, Pallas kernels: none -> 68.1 us  [the longest x2 43.1 us: on_device(): pl.pallas_call(lambda *refs, slots=slots, first=first: rank_kernel(slots,...]
    all_to_all x0 -> x2, blocking collectives: none -> 61.9 us  [all_to_all(): return lax.all_to_all(v, 'own', split_axis=0, concat_axis=0, tiled=True)]
    another operation x2 -> x0, other arithmetic: 18 us -> none
    unnamed x39 -> x4, local copies, waits for them, and re-layouts: 17.1 us -> 1.35 us
    convert_element_type x2 -> x0, local copies, waits for them, and re-layouts: 14.1 us -> none  [attend(): return (acc.reshape(total, width) / counts[:, None]).astype(jnp.bfloat16)]
    all_to_all x2 -> x1, starting transfers between devices: 17.7 us -> 4.87 us  [all_to_all(): return lax.all_to_all(v, 'own', split_axis=0, concat_axis=0, tiled=True)]
  transfers between devices with their start and end apart: 2 -> 1, of which waited for: 2 -> 0; matrix products, arithmetic and copies ran while one was open for 12% -> 0% of each run, Pallas kernels for 0% -> 24%
where the time goes in v1:
time: 139 us; the launch traced here: 138 us
  Pallas kernels  68.1 us (49%)
  blocking collectives  61.9 us (45%)
  starting transfers between devices  4.87 us (4%)
    all_to_all x2, blocking collectives, all_to_all(): return lax.all_to_all(v, 'own', split_axis=0, concat_axis=0, tiled=True)  61.9 us
    pallas_call x2, Pallas kernels, on_device(): pl.pallas_call(lambda *refs, slots=slots, first=first: rank_kernel(slots,...  43.1 us
    pallas_call x1, Pallas kernels, on_device(): pl.pallas_call(new_kernel, out_shape=(sds((total, width), BF), sds((total...  11.3 us
    pallas_call x1, Pallas kernels, on_device(): pl.pallas_call(lambda *refs: route_kernel(chunks[0], *refs), out_shape=(s...  6.62 us
    pallas_call x1, Pallas kernels, on_device(): pl.pallas_call(lambda *refs, slots=slots, first=first: fill_kernel(slots,...  5.25 us
    all_to_all x1, starting transfers between devices, all_to_all(): return lax.all_to_all(v, 'own', split_axis=0, concat_axis=0, tiled=True)  4.87 us
  transfers between devices with their start and end apart: 1, of which 0 were waited for; matrix products, arithmetic and copies ran while one was open for 0% of the time, Pallas kernels for 24%

profile of v1, /device:TPU:0, one launch (start us, length us, event | category | flops | bytes accessed | tf_op | source)
XLA Modules:
  0.0 138.2 jit_solution(14660310882399292946)
XLA Ops:
  0.6 6.6 %route.1 = (bf16[1024,1024]{1,0:T(8,128)(2,1)}, bf16[1024,1024]{1,0:T(8,128)(2,1)}, s32[2,1024]{1,0:T(2,128)}, f32[1,1024]{1,0:T(1,128)}) custom-call(bf16[1024,1024]{1,0:T(8,128)(2,1)} %refs_0_.3, s32[1,1024]{1,0:T(1,128)} %bitcast.28, s32[1,64]{1,0:T(1,128)} %bitcast.29, f32[1,1024]{1,0:T(1,128)} %bitcast.24), custom_call_target="tpu_custom_call" | custom-call | flops 2147483648 | bytes 6291456 | tf_op jit(solution)/shard_map/route/pallas_call | solution.py:207
  7.3 5.2 %fill.1 = bf16[1024,1024]{1,0:T(8,128)(2,1)} custom-call(s32[2,1024]{1,0:T(2,128)} %get-tuple-element.10.refs_0_.place_ref, bf16[1024,1024]{1,0:T(8,128)(2,1)} %get-tuple-element.16.refs_1_), custom_call_target="tpu_custom_call" | custom-call | flops 2147483648 | bytes 4194304 | tf_op jit(solution)/shard_map/fill/pallas_call | solution.py:225
  12.5 42.1 %all_to_all.15 = bf16[64,16,1024]{2,1,0:T(8,128)(2,1)} all-to-all(bf16[64,16,1024]{2,1,0:T(8,128)(2,1)} %bitcast.20), channel_id=1, replica_groups=mesh['grp'=2,'own'=64] {'own'}, dimensions={0} | all-to-all | bytes 4194304 | tf_op jit(solution)/shard_map/all_to_all | solution.py:205
  54.6 4.9 %all-to-all-start = ((bf16[64,16,1024]{2,1,0:T(8,128)(2,1)}), bf16[64,16,1024]{2,1,0:T(8,128)(2,1)S(1)}, u32[]{:S(2)}, u32[]{:S(2)}) async-start(bf16[64,16,1024]{2,1,0:T(8,128)(2,1)} %bitcast.3), calls=%async_computation | async-start | bytes 4194304 | tf_op jit(solution)/shard_map/all_to_all | solution.py:205
  60.1 11.3 %fresh.1 = (bf16[1088,1024]{1,0:T(8,128)(2,1)}, bf16[1088,1024]{1,0:T(8,128)(2,1)}, bf16[8,1024]{1,0:T(8,128)(2,1)}, bf16[64,1024]{1,0:T(8,128)(2,1)}) custom-call(s32[1]{0:T(128)S(6)} %copy.13.length_ref.refs_0_, bf16[64,1024]{1,0:T(8,128)(2,1)} %bitcast.21, bf16[1024,4096]{1,0:T(8,128)(2,1)} %refs_3_.3, bf16[1024,1024]{1,0:T(8,128)(2,1)} %bitcast.16, ...), custom_call_target="tpu_custom_call" | custom-call | flops 1073741824 | bytes 20971520 | tf_op jit(solution)/shard_map/fresh/pallas_call | solution.py:237
  71.4 21.6 %rank.3 = f32[64,128]{1,0:T(8,128)} custom-call(s32[1]{0:T(128)S(6)} %copy.13.length_ref.refs_0_, bf16[1024,1024]{1,0:T(8,128)(2,1)} %bitcast.19, bf16[1024,4096]{1,0:T(8,128)(2,1)} %refs_3_.3, bf16[1024,4096]{1,0:T(8,128)(2,1)} %refs_3_.3, bf16[1088,1024]{1,0:T(8,128)(2,1)} %get-tuple-element.13.refs_4_, bf16[1088,1024]{1,0:T(8,128)(2,1)} %get-tuple-element.14.refs_5_, ...), custom_call_target="tpu_custom_call" | custom-call | flops 13421772800 | bytes 10485760 | tf_op jit(solution)/shard_map/rank/pallas_call | solution.py:257
  93.0 0.0 all-to-all-done
  93.0 0.0 copy-start
  93.0 1.3 copy-done
  94.4 0.0 copy-start.1
  94.4 21.6 %rank.2 = f32[64,128]{1,0:T(8,128)} custom-call(s32[1]{0:T(128)S(6)} %copy.13.length_ref.refs_0_, bf16[1024,1024]{1,0:T(8,128)(2,1)} %bitcast.18, bf16[1024,4096]{1,0:T(8,128)(2,1)} %refs_3_.3, bf16[1024,4096]{1,0:T(8,128)(2,1)} %refs_3_.3, bf16[1088,1024]{1,0:T(8,128)(2,1)} %get-tuple-element.13.refs_4_, bf16[1088,1024]{1,0:T(8,128)(2,1)} %get-tuple-element.14.refs_5_, ...), custom_call_target="tpu_custom_call" | custom-call | flops 13421772800 | bytes 10485760 | tf_op jit(solution)/shard_map/rank/pallas_call | solution.py:257
  115.9 0.0 copy-done.1
  115.9 0.8 add.3
  116.7 19.8 %all_to_all.16 = f32[64,1,128]{2,1,0:T(1,128)} all-to-all(f32[64,1,128]{2,1,0:T(1,128)S(1)} %bitcast.22), channel_id=1, replica_groups=mesh['grp'=2,'own'=64] {'own'}, dimensions={0} | all-to-all | bytes 65536 | tf_op jit(solution)/shard_map/all_to_all | solution.py:205
  136.4 1.8 %scores.1 = f32[1,1024]{1,0:T(1,128)} custom-call(s32[2,1024]{1,0:T(2,128)} %get-tuple-element.10.refs_0_.place_ref, f32[1,1024]{1,0:T(1,128)} %get-tuple-element.11.base_ref, f32[64,128]{1,0:T(8,128)} %bitcast.23), custom_call_target="tpu_custom_call" | custom-call | tf_op jit(solution)/shard_map/scores/pallas_call | solution.py:281
Async XLA Ops:
  54.6 38.4 %all-to-all-start = ((bf16[64,16,1024]{2,1,0:T(8,128)(2,1)}), bf16[64,16,1024]{2,1,0:T(8,128)(2,1)S(1)}, u32[]{:S(2)}, u32[]{:S(2)}) async-start(bf16[64,16,1024]{2,1,0:T(8,128)(2,1)} %bitcast.3), calls=%async_computation | async-start | bytes 4194304 | tf_op jit(solution)/shard_map/all_to_all | solution.py:205
  93.0 1.3 copy-start
  94.4 21.6 %copy-start.1 = (f32[64,128]{1,0:T(8,128)S(1)}, f32[64,128]{1,0:T(8,128)}, u32[]{:S(2)}) copy-start(f32[64,128]{1,0:T(8,128)} %rank.3) | copy-start | bytes 98308
